TPU v7x, 32 devices: a whole 2x2x4 slice. The times are simulated.
32 devices in a mesh: seq: 16 (over z, y, core), head: 2 (over x).
Axes of the slice: x: 2, y: 2, z: 4, core: 2. Of those that a mesh axis runs over, the one named last changes fastest.
Arguments:
- embedded: bfloat16 [4096, 1536], P('seq', 'head'), may hold values from -27 to 27
- grad_out: bfloat16 [4096, 1536], P('seq', 'head'), may hold values from -6 to 6
- mask_pos: int32 [608], P('seq'), may hold values from 0 to 4095, as said below
- timestep: int32 [1], replicated, may hold values from 0 to 999
- time_table: bfloat16 [1000, 1536], replicated, may hold values from -3 to 3
- mask_embed: bfloat16 [1536], replicated, may hold values from -6 to 6
- w_query: bfloat16 [1536, 768], P(None, 'head'), may hold values from -0.15625 to 0.15625
- w_key: bfloat16 [1536, 768], P(None, 'head'), may hold values from -0.15625 to 0.15625
- w_value: bfloat16 [1536, 768], P(None, 'head'), may hold values from -0.15625 to 0.15625
- w_out: bfloat16 [768, 1536], P('head'), may hold values from -0.21875 to 0.21875
Outputs:
- input_grad: bfloat16 [4096, 1536], P('seq', 'head')
- query_weight_grad: float32 [1536, 768], P('seq', 'head')
- key_weight_grad: float32 [1536, 768], P('seq', 'head')
- value_weight_grad: float32 [1536, 768], P('seq', 'head')
- out_weight_grad: float32 [1536, 768], P('seq', 'head')
Inputs may be any that keep to these rules, and one draw needn't show every extreme that they name: `mask_pos`: the entries are distinct; entries b * 38 to (b + 1) * 38 - 1 lie in positions b * 256 to (b + 1) * 256 - 1.
All inputs are finite; a program needn't handle non-finite values.
Results may differ from a plain program's by a relative error of at most 0.01.
The roundings to bfloat16 on the way count: a program that leaves them out, or rounds other values in their place, can miss the bound.
Values may be sent and summed in bfloat16 or wider, within the bound.
A program may use at most 128 MiB of HBM per device.

v0:
```python
import jax
import jax.numpy as jnp
from jax import lax
from jax.sharding import PartitionSpec as P

HEAD_DIM = 64
HALF = 1024


NEG_FILL = -1e30


def passed_along(value, axis, steps):
    count = lax.axis_size(axis)
    first, last = (max(0, -steps), min(count, count - steps))
    return lax.ppermute(value, axis, [(source, source + steps) for source in range(first, last)])


def contract_first(left, right):
    return lax.dot_general(
        left, right, (((0,), (0,)), ((), ())), preferred_element_type=jnp.float32
    )


def contract_last(left, right):
    return lax.dot_general(
        left, right, (((1,), (1,)), ((), ())), preferred_element_type=jnp.float32
    )


def body(
    embedded, grad_out, mask_pos, timestep, time_table, mask_embed, w_query, w_key, w_value, w_out
):
    full_rows, full_grad = (
        lax.all_gather(embedded, "head", axis=1, tiled=True),
        lax.all_gather(grad_out, "head", axis=1, tiled=True),
    )
    slab_rows = full_rows.shape[0]
    seq_index = lax.axis_index("seq")
    seq_count = lax.axis_size("seq")
    reach = HALF // slab_rows
    total_len = slab_rows * seq_count
    span = slab_rows * (2 * reach + 1)
    scale = HEAD_DIM ** (-0.5)
    positions = seq_index * slab_rows + jnp.arange(slab_rows, dtype=jnp.int32)
    masked = jnp.any(positions[:, None] == mask_pos[None, :], axis=1)
    time_row = lax.dynamic_slice_in_dim(time_table, timestep[0], 1, 0).astype(jnp.float32)
    hidden = (
        jnp.where(
            masked[:, None], mask_embed.astype(jnp.float32)[None, :], full_rows.astype(jnp.float32)
        )
        + time_row
    ).astype(jnp.bfloat16)
    queries = jnp.dot(hidden, w_query, preferred_element_type=jnp.float32).astype(jnp.bfloat16)
    key_rows = jnp.dot(hidden, w_key, preferred_element_type=jnp.float32).astype(jnp.bfloat16)
    value_rows = jnp.dot(hidden, w_value, preferred_element_type=jnp.float32).astype(jnp.bfloat16)
    grad_attn = contract_last(full_grad, w_out).astype(jnp.bfloat16)
    group_width = queries.shape[1]
    head_count = group_width // HEAD_DIM
    lower_parts = []
    moving = (key_rows, value_rows)
    for distance in range(reach):
        moving = passed_along((moving[0], moving[1]), "seq", 1)
        lower_parts.insert(0, moving)
    upper_parts = []
    moving = (key_rows, value_rows)
    for distance in range(reach):
        moving = passed_along((moving[0], moving[1]), "seq", -1)
        upper_parts.append(moving)
    slabs = lower_parts + [(key_rows, value_rows)] + upper_parts
    keys_all = jnp.concatenate([pair[0] for pair in slabs], axis=0)
    values_all = jnp.concatenate([pair[1] for pair in slabs], axis=0)
    key_pos = (seq_index - reach) * slab_rows + jnp.arange(span, dtype=jnp.int32)
    distance_grid = positions[:, None] - key_pos[None, :]
    band = (
        (jnp.abs(distance_grid) <= HALF) & (key_pos[None, :] >= 0) & (key_pos[None, :] < total_len)
    )
    attentions = []
    head_outputs = []
    for head_index in range(head_count):
        lower_col = head_index * HEAD_DIM
        upper_col = lower_col + HEAD_DIM
        head_query = queries[:, lower_col:upper_col]
        head_keys = keys_all[:, lower_col:upper_col]
        head_values = values_all[:, lower_col:upper_col]
        scores = contract_last(head_query, head_keys) * scale
        scores = jnp.where(band, scores, NEG_FILL)
        row_max = jnp.max(scores, axis=1, keepdims=True)
        log_total = row_max + jnp.log(jnp.sum(jnp.exp(scores - row_max), axis=1, keepdims=True))
        attention = jnp.exp(scores - log_total)
        rounded = attention.astype(jnp.bfloat16)
        head_outputs.append(
            jnp.dot(rounded, head_values, preferred_element_type=jnp.float32).astype(jnp.bfloat16)
        )
        attentions.append(attention)
    attn_out = jnp.concatenate(head_outputs, axis=1)
    query_grads = []
    key_grads = []
    value_grads = []
    for head_index in range(head_count):
        lower_col = head_index * HEAD_DIM
        upper_col = lower_col + HEAD_DIM
        head_query = queries[:, lower_col:upper_col]
        head_keys = keys_all[:, lower_col:upper_col]
        head_values = values_all[:, lower_col:upper_col]
        head_grad = grad_attn[:, lower_col:upper_col]
        attention = attentions[head_index]
        rounded = attention.astype(jnp.bfloat16)
        delta = jnp.sum(
            head_grad.astype(jnp.float32) * head_outputs[head_index].astype(jnp.float32), axis=1
        )
        dprob = contract_last(head_grad, head_values)
        dscore = (attention * (dprob - delta[:, None])).astype(jnp.bfloat16)
        query_grads.append(scale * jnp.dot(dscore, head_keys, preferred_element_type=jnp.float32))
        key_grads.append(scale * contract_first(dscore, head_query))
        value_grads.append(contract_first(rounded, head_grad))
    query_grad = jnp.concatenate(query_grads, axis=1)
    key_grad_all = jnp.concatenate(key_grads, axis=1)
    value_grad_all = jnp.concatenate(value_grads, axis=1)

    def slab_of(array, slab_index):
        return array[slab_index * slab_rows : (slab_index + 1) * slab_rows]

    carried = (slab_of(key_grad_all, 2 * reach), slab_of(value_grad_all, 2 * reach))
    for step_index in range(1, reach + 1):
        arrived = passed_along((carried[0], carried[1]), "seq", 1)
        source = 2 * reach - step_index
        carried = (
            arrived[0] + slab_of(key_grad_all, source),
            arrived[1] + slab_of(value_grad_all, source),
        )
    carried_low = (slab_of(key_grad_all, 0), slab_of(value_grad_all, 0))
    for step_index in range(1, reach + 1):
        arrived = passed_along((carried_low[0], carried_low[1]), "seq", -1)
        if step_index < reach:
            carried_low = (
                arrived[0] + slab_of(key_grad_all, step_index),
                arrived[1] + slab_of(value_grad_all, step_index),
            )
        else:
            carried_low = arrived
    key_total = carried[0] + carried_low[0]
    value_total = carried[1] + carried_low[1]
    query_rounded = query_grad.astype(jnp.bfloat16)
    key_rounded = key_total.astype(jnp.bfloat16)
    value_rounded = value_total.astype(jnp.bfloat16)
    stacked = jnp.concatenate([query_rounded, key_rounded, value_rounded], axis=1)
    merged = lax.psum_scatter(
        jnp.concatenate(
            [contract_first(hidden, stacked), contract_first(full_grad, attn_out)], axis=1
        ),
        "seq",
        scatter_dimension=0,
        tiled=True,
    )
    proj_grad = merged[:, : 3 * group_width]
    out_weight_grad = merged[:, 3 * group_width :]
    query_weight_grad = proj_grad[:, :group_width]
    key_weight_grad = proj_grad[:, group_width : 2 * group_width]
    value_weight_grad = proj_grad[:, 2 * group_width :]
    partial_grad = contract_last(query_rounded, w_query)
    partial_grad = partial_grad + contract_last(key_rounded, w_key)
    partial_grad = partial_grad + contract_last(value_rounded, w_value)
    summed = lax.psum_scatter(partial_grad, "head", scatter_dimension=1, tiled=True)
    input_grad = jnp.where(masked[:, None], 0.0, summed).astype(jnp.bfloat16)
    return (input_grad, query_weight_grad, key_weight_grad, value_weight_grad, out_weight_grad)


def solution(mesh):
    placed = (
        P("seq", "head"),
        P("seq", "head"),
        P("seq"),
        P(),
        P(),
        P(),
        P(None, "head"),
        P(None, "head"),
        P(None, "head"),
        P("head", None),
    )
    return jax.shard_map(
        body,
        mesh=mesh,
        in_specs=placed,
        out_specs=(
            P("seq", "head"),
            P("seq", "head"),
            P("seq", "head"),
            P("seq", "head"),
            P("seq", "head"),
        ),
        check_vma=False,
    )
```

profile of v0, /device:TPU:0, one launch (start us, length us, event | category | flops | bytes accessed | tf_op | source)
XLA Modules:
  0.0 351.9 jit_solution(3299947537823519173)
XLA Ops:
  8.7 13.0 %all_gather.6 = bf16[256,1536]{1,0:T(8,128)(2,1)S(1)} all-gather(bf16[256,768]{1,0:T(8,128)(2,1)} %param.10), channel_id=1, replica_groups=mesh['seq'=16,'head'=2] {'head'}, dimensions={1}, use_global_device_ids=true | all-gather | bytes 1179648 | tf_op jit(solution)/shard_map/all_gather | solution.py:35
  23.3 1.9 convolution_convert_fusion
  25.2 1.3 collective-permute-start.12
  26.5 3.7 %collective-permute-start.8 = (bf16[256,384]{1,0:T(8,128)(2,1)S(1)}, bf16[256,384]{1,0:T(8,128)(2,1)}, u32[]{:S(2)}, u32[]{:S(2)}) collective-permute-start(bf16[256,384]{1,0:T(8,128)(2,1)S(1)} %convolution_convert_fusion), channel_id=1, source_target_pairs={{0,2},{2,4},{4,6},{6,8},{8,10},{10,12},{12,14},{14,16},{16,18},{18... | collective-permute-start | bytes 589832 | tf_op jit(solution)/shard_map/ppermute | solution.py:16
  30.9 1.4 collective-permute-start.4
  32.3 3.2 collective-permute-start
  36.6 6.3 %collective-permute-start.1 = (bf16[256,384]{1,0:T(8,128)(2,1)S(1)}, bf16[256,384]{1,0:T(8,128)(2,1)S(1)}, u32[]{:S(2)}, u32[]{:S(2)}) collective-permute-start(bf16[256,384]{1,0:T(8,128)(2,1)S(1)} %collective-permute-done), channel_id=1, source_target_pairs={{0,2},{2,4},{4,6},{6,8},{8,10},{10,12},{12,14},{14,16},{16,18},{18... | collective-permute-start | bytes 589832 | tf_op jit(solution)/shard_map/ppermute | solution.py:16
  43.6 1.3 collective-permute-start.13
  44.9 5.0 %collective-permute-start.9 = (bf16[256,384]{1,0:T(8,128)(2,1)}, bf16[256,384]{1,0:T(8,128)(2,1)S(1)}, u32[]{:S(2)}, u32[]{:S(2)}) collective-permute-start(bf16[256,384]{1,0:T(8,128)(2,1)} %collective-permute-done.8), channel_id=1, source_target_pairs={{0,2},{2,4},{4,6},{6,8},{8,10},{10,12},{12,14},{14,16},{16,18},{18... | collective-permute-start | bytes 589832 | tf_op jit(solution)/shard_map/ppermute | solution.py:16
  49.9 1.3 collective-permute-start.5
  51.3 4.3 %collective-permute-start.2 = (bf16[256,384]{1,0:T(8,128)(2,1)S(1)}, bf16[256,384]{1,0:T(8,128)(2,1)S(1)}, u32[]{:S(2)}, u32[]{:S(2)}) collective-permute-start(bf16[256,384]{1,0:T(8,128)(2,1)S(1)} %collective-permute-done.1), channel_id=1, source_target_pairs={{0,2},{2,4},{4,6},{6,8},{8,10},{10,12},{12,14},{14,16},{16,18},{18... | collective-permute-start | bytes 589832 | tf_op jit(solution)/shard_map/ppermute | solution.py:16
  55.6 12.1 %all_gather.7 = bf16[256,1536]{1,0:T(8,128)(2,1)S(1)} all-gather(bf16[256,768]{1,0:T(8,128)(2,1)S(1)} %copy-done.4), channel_id=1, replica_groups=mesh['seq'=16,'head'=2] {'head'}, dimensions={1}, use_global_device_ids=true | all-gather | bytes 1179648 | tf_op jit(solution)/shard_map/all_gather | solution.py:36
  69.0 3.1 collective-permute-start.10
  72.1 1.3 collective-permute-start.6
  73.4 4.3 %collective-permute-start.3 = (bf16[256,384]{1,0:T(8,128)(2,1)S(1)}, bf16[256,384]{1,0:T(8,128)(2,1)S(1)}, u32[]{:S(2)}, u32[]{:S(2)}) collective-permute-start(bf16[256,384]{1,0:T(8,128)(2,1)S(1)} %collective-permute-done.2), channel_id=1, source_target_pairs={{0,2},{2,4},{4,6},{6,8},{8,10},{10,12},{12,14},{14,16},{16,18},{18... | collective-permute-start | bytes 589832 | tf_op jit(solution)/shard_map/ppermute | solution.py:16
  78.3 1.3 collective-permute-start.15
  79.6 4.3 %collective-permute-start.11 = (bf16[256,384]{1,0:T(8,128)(2,1)S(1)}, bf16[256,384]{1,0:T(8,128)(2,1)S(1)}, u32[]{:S(2)}, u32[]{:S(2)}) collective-permute-start(bf16[256,384]{1,0:T(8,128)(2,1)S(1)} %collective-permute-done.10), channel_id=1, source_target_pairs={{0,2},{2,4},{4,6},{6,8},{8,10},{10,12},{12,14},{14,16},{16,18},{18... | collective-permute-start | bytes 589832 | tf_op jit(solution)/shard_map/ppermute | solution.py:16
  83.9 1.5 collective-permute-start.7
  86.6 2.4 collective-permute-done.7
  104.5 1.5 multiply_reduce_fusion
  114.4 7.0 %collective-permute-start.24 = (f32[256,384]{0,1:T(8,128)S(1)}, f32[256,384]{0,1:T(8,128)S(1)}, u32[]{:S(2)}, u32[]{:S(2)}) collective-permute-start(f32[256,384]{0,1:T(8,128)S(1)} %get-tuple-element.36), channel_id=1, source_target_pairs={{0,2},{2,4},{4,6},{6,8},{8,10},{10,12},{12,14},{14,16},{16,18},{18... | collective-permute-start | bytes 1179656 | tf_op jit(solution)/shard_map/ppermute | solution.py:16
  121.4 1.3 collective-permute-start.28
  124.9 3.1 collective-permute-start.16
  127.9 1.3 collective-permute-start.20
  129.2 1.4 constant_dynamic-update-slice_fusion.30
  131.7 1.4 constant_dynamic-update-slice_fusion.28
  133.1 2.6 collective-permute-done.20
  135.9 7.9 %collective-permute-start.17 = (f32[256,384]{0,1:T(8,128)S(1)}, f32[256,384]{0,1:T(8,128)S(1)}, u32[]{:S(2)}, u32[]{:S(2)}) collective-permute-start(f32[256,384]{0,1:T(8,128)S(1)} %get-tuple-element.42), channel_id=1, source_target_pairs={{0,2},{2,4},{4,6},{6,8},{8,10},{10,12},{12,14},{14,16},{16,18},{18... | collective-permute-start | bytes 1179656 | tf_op jit(solution)/shard_map/ppermute | solution.py:16
  143.8 1.6 collective-permute-start.21
  146.6 3.1 collective-permute-start.25
  149.6 1.3 collective-permute-start.29
  151.1 5.6 %collective-permute-start.18 = (f32[256,384]{0,1:T(8,128)S(1)}, f32[256,384]{0,1:T(8,128)S(1)}, u32[]{:S(2)}, u32[]{:S(2)}) collective-permute-start(f32[256,384]{0,1:T(8,128)S(1)} %get-tuple-element.40), channel_id=1, source_target_pairs={{0,2},{2,4},{4,6},{6,8},{8,10},{10,12},{12,14},{14,16},{16,18},{18... | collective-permute-start | bytes 1179656 | tf_op jit(solution)/shard_map/ppermute | solution.py:16
  156.7 1.3 collective-permute-start.22
  158.0 1.4 constant_dynamic-update-slice_fusion.26
  159.5 6.0 %collective-permute-start.26 = (f32[256,384]{0,1:T(8,128)S(1)}, f32[256,384]{0,1:T(8,128)S(1)}, u32[]{:S(2)}, u32[]{:S(2)}) collective-permute-start(f32[256,384]{0,1:T(8,128)S(1)} %get-tuple-element.32), channel_id=1, source_target_pairs={{0,2},{2,4},{4,6},{6,8},{8,10},{10,12},{12,14},{14,16},{16,18},{18... | collective-permute-start | bytes 1179656 | tf_op jit(solution)/shard_map/ppermute | solution.py:16
  166.9 7.0 %collective-permute-start.19 = (f32[256,384]{0,1:T(8,128)S(1)}, f32[256,384]{0,1:T(8,128)S(1)}, u32[]{:S(2)}, u32[]{:S(2)}) collective-permute-start(f32[256,384]{0,1:T(8,128)S(1)} %get-tuple-element.38), channel_id=1, source_target_pairs={{0,2},{2,4},{4,6},{6,8},{8,10},{10,12},{12,14},{14,16},{16,18},{18... | collective-permute-start | bytes 1179656 | tf_op jit(solution)/shard_map/ppermute | solution.py:16
  176.0 6.4 %collective-permute-start.27 = (f32[256,384]{0,1:T(8,128)S(1)}, f32[256,384]{0,1:T(8,128)S(1)}, u32[]{:S(2)}, u32[]{:S(2)}) collective-permute-start(f32[256,384]{0,1:T(8,128)S(1)} %get-tuple-element.30), channel_id=1, source_target_pairs={{0,2},{2,4},{4,6},{6,8},{8,10},{10,12},{12,14},{14,16},{16,18},{18... | collective-permute-start | bytes 1179656 | tf_op jit(solution)/shard_map/ppermute | solution.py:16
  182.3 1.3 collective-permute-start.31
  185.0 2.9 collective-permute-done.31
  188.6 1.8 convolution_add_fusion
  191.4 1.4 convolution_bitcast_fusion
  192.8 5.2 %fusion.104 = f32[1536,1152]{0,1:T(8,128)} fusion(bf16[256,1152]{0,1:T(8,128)(2,1)} %get-tuple-element.26, bf16[256,1536]{1,0:T(8,128)(2,1)S(1)} %all_gather.6, f32[1536]{0:T(1024)S(1)} %convert_reduce_fusion, f32[1536]{0:T(1024)S(1)} %convert_element_type.128, pred[256]{0:T(512)(128)(4,1)S(1)} %compare_reduce_fusion), kind=kOutput, calls=%fused_computation.213 | convolution fusion | flops 907542528 | bytes 8466688 | tf_op jit(solution)/shard_map/dot_general | solution.py:20
  198.0 7.8 %pad_maximum_fusion = f32[1536,1536]{0,1:T(8,128)} fusion(f32[1536,384]{0,1:T(8,128)S(1)} %convolution_bitcast_fusion, f32[1536,1152]{0,1:T(8,128)} %fusion.104), kind=kLoop, calls=%fused_computation | loop fusion | flops 2359296 | bytes 18874368 | tf_op jit(solution)/shard_map/concatenate | solution.py:149
  205.8 10.0 %copy.51 = f32[1536,1536]{1,0:T(8,128)} copy(f32[1536,1536]{0,1:T(8,128)} %pad_maximum_fusion) | data formatting | bytes 18874368
  215.7 11.3 %reduce-scatter.5.cloned.1.call-done = f32[256,768]{1,0:T(8,128)} async-done(((f32[256,1536]{1,0:T(8,128)}), f32[256,768]{1,0:T(8,128)}) %reduce-scatter.5.cloned.1.call-update) | async-done | bytes 786448 | tf_op jit(solution)/shard_map/reduce_scatter | solution.py:164
  227.1 2.0 select_convert_fusion
  229.1 114.1 %reduce-scatter.7.cloned.1.call-done = f32[96,1536]{1,0:T(8,128)} async-done(((f32[1536,1536]{1,0:T(8,128)}), f32[96,1536]{1,0:T(8,128)}) %reduce-scatter.7.cloned.1.call-update) | async-done | bytes 589840
  343.1 1.9 fusion.109
  (146 shorter events, 42.8 us)
Async XLA Ops:
  7.2 35.8 %copy-start = (bf16[1536,384]{1,0:T(8,128)(2,1)S(1)}, bf16[1536,384]{1,0:T(8,128)(2,1)}, u32[]{:S(2)}) copy-start(bf16[1536,384]{1,0:T(8,128)(2,1)} %param.16) | copy-start | bytes 3538948
  7.2 219.9 %reduce-scatter.5.cloned.1.call-start = ((), (), s32[]{:S(2)}) async-start(), calls=%async_computation.2 | async-start | bytes 2359296 | tf_op jit(solution)/shard_map/reduce_scatter | solution.py:164
  22.4 7.8 %copy-start.1 = (bf16[1536,384]{1,0:T(8,128)(2,1)S(1)}, bf16[1536,384]{1,0:T(8,128)(2,1)}, u32[]{:S(2)}) copy-start(bf16[1536,384]{1,0:T(8,128)(2,1)} %param.17) | copy-start | bytes 3538948
  25.2 18.4 %copy-start.6 = (bf16[256,384]{1,0:T(8,128)(2,1)}, bf16[256,384]{1,0:T(8,128)(2,1)S(1)}, u32[]{:S(2)}) copy-start(bf16[256,384]{1,0:T(8,128)(2,1)S(1)} %convolution_convert_fusion) | copy-start | bytes 589828
  25.2 18.4 %collective-permute-start.12 = (bf16[256,384]{1,0:T(8,128)(2,1)S(1)}, bf16[256,384]{1,0:T(8,128)(2,1)S(1)}, u32[]{:S(2)}, u32[]{:S(2)}) collective-permute-start(bf16[256,384]{1,0:T(8,128)(2,1)S(1)} %convolution_convert_fusion), channel_id=1, source_target_pairs={{2,0},{4,2},{6,4},{8,6},{10,8},{12,10},{14,12},{16,14},{18,16},{20... | collective-permute-start | bytes 589832 | tf_op jit(solution)/shard_map/ppermute | solution.py:16
  26.5 18.4 %collective-permute-start.8 = (bf16[256,384]{1,0:T(8,128)(2,1)S(1)}, bf16[256,384]{1,0:T(8,128)(2,1)}, u32[]{:S(2)}, u32[]{:S(2)}) collective-permute-start(bf16[256,384]{1,0:T(8,128)(2,1)S(1)} %convolution_convert_fusion), channel_id=1, source_target_pairs={{0,2},{2,4},{4,6},{6,8},{8,10},{10,12},{12,14},{14,16},{16,18},{18... | collective-permute-start | bytes 589832 | tf_op jit(solution)/shard_map/ppermute | solution.py:16
  30.8 20.4 %copy-start.8 = (bf16[256,384]{1,0:T(8,128)(2,1)}, bf16[256,384]{1,0:T(8,128)(2,1)S(1)}, u32[]{:S(2)}) copy-start(bf16[256,384]{1,0:T(8,128)(2,1)S(1)} %convolution_convert_fusion.2) | copy-start | bytes 589828
  30.8 24.7 %copy-start.4 = (bf16[256,768]{1,0:T(8,128)(2,1)S(1)}, bf16[256,768]{1,0:T(8,128)(2,1)}, u32[]{:S(2)}) copy-start(bf16[256,768]{1,0:T(8,128)(2,1)} %param.11) | copy-start | bytes 1179652
  30.9 19.1 %collective-permute-start.4 = (bf16[256,384]{1,0:T(8,128)(2,1)S(1)}, bf16[256,384]{1,0:T(8,128)(2,1)}, u32[]{:S(2)}, u32[]{:S(2)}) collective-permute-start(bf16[256,384]{1,0:T(8,128)(2,1)S(1)} %convolution_convert_fusion.2), channel_id=1, source_target_pairs={{2,0},{4,2},{6,4},{8,6},{10,8},{12,10},{14,12},{16,14},{18,16},{20... | collective-permute-start | bytes 589832 | tf_op jit(solution)/shard_map/ppermute | solution.py:16
  32.3 4.3 %collective-permute-start = (bf16[256,384]{1,0:T(8,128)(2,1)S(1)}, bf16[256,384]{1,0:T(8,128)(2,1)S(1)}, u32[]{:S(2)}, u32[]{:S(2)}) collective-permute-start(bf16[256,384]{1,0:T(8,128)(2,1)S(1)} %convolution_convert_fusion.2), channel_id=1, source_target_pairs={{0,2},{2,4},{4,6},{6,8},{8,10},{10,12},{12,14},{14,16},{16,18},{18... | collective-permute-start | bytes 589832 | tf_op jit(solution)/shard_map/ppermute | solution.py:16
  35.5 42.1 %copy-start.12 = (bf16[384,1536]{1,0:T(8,128)(2,1)S(1)}, bf16[384,1536]{1,0:T(8,128)(2,1)}, u32[]{:S(2)}) copy-start(bf16[384,1536]{1,0:T(8,128)(2,1)} %param.19) | copy-start | bytes 3538948
  36.6 14.7 %copy-start.10 = (bf16[256,384]{1,0:T(8,128)(2,1)}, bf16[256,384]{1,0:T(8,128)(2,1)S(1)}, u32[]{:S(2)}) copy-start(bf16[256,384]{1,0:T(8,128)(2,1)S(1)} %collective-permute-done) | copy-start | bytes 589828
  36.6 14.7 %collective-permute-start.1 = (bf16[256,384]{1,0:T(8,128)(2,1)S(1)}, bf16[256,384]{1,0:T(8,128)(2,1)S(1)}, u32[]{:S(2)}, u32[]{:S(2)}) collective-permute-start(bf16[256,384]{1,0:T(8,128)(2,1)S(1)} %collective-permute-done), channel_id=1, source_target_pairs={{0,2},{2,4},{4,6},{6,8},{8,10},{10,12},{12,14},{14,16},{16,18},{18... | collective-permute-start | bytes 589832 | tf_op jit(solution)/shard_map/ppermute | solution.py:16
  43.6 24.1 %collective-permute-start.13 = (bf16[256,384]{1,0:T(8,128)(2,1)S(1)}, bf16[256,384]{1,0:T(8,128)(2,1)S(1)}, u32[]{:S(2)}, u32[]{:S(2)}) collective-permute-start(bf16[256,384]{1,0:T(8,128)(2,1)S(1)} %collective-permute-done.12), channel_id=1, source_target_pairs={{2,0},{4,2},{6,4},{8,6},{10,8},{12,10},{14,12},{16,14},{18,16},{20... | collective-permute-start | bytes 589832 | tf_op jit(solution)/shard_map/ppermute | solution.py:16
  44.9 24.1 %collective-permute-start.9 = (bf16[256,384]{1,0:T(8,128)(2,1)}, bf16[256,384]{1,0:T(8,128)(2,1)S(1)}, u32[]{:S(2)}, u32[]{:S(2)}) collective-permute-start(bf16[256,384]{1,0:T(8,128)(2,1)} %collective-permute-done.8), channel_id=1, source_target_pairs={{0,2},{2,4},{4,6},{6,8},{8,10},{10,12},{12,14},{14,16},{16,18},{18... | collective-permute-start | bytes 589832 | tf_op jit(solution)/shard_map/ppermute | solution.py:16
  49.9 22.1 %collective-permute-start.5 = (bf16[256,384]{1,0:T(8,128)(2,1)}, bf16[256,384]{1,0:T(8,128)(2,1)S(1)}, u32[]{:S(2)}, u32[]{:S(2)}) collective-permute-start(bf16[256,384]{1,0:T(8,128)(2,1)} %collective-permute-done.4), channel_id=1, source_target_pairs={{2,0},{4,2},{6,4},{8,6},{10,8},{12,10},{14,12},{16,14},{18,16},{20... | collective-permute-start | bytes 589832 | tf_op jit(solution)/shard_map/ppermute | solution.py:16
  51.3 22.1 %collective-permute-start.2 = (bf16[256,384]{1,0:T(8,128)(2,1)S(1)}, bf16[256,384]{1,0:T(8,128)(2,1)S(1)}, u32[]{:S(2)}, u32[]{:S(2)}) collective-permute-start(bf16[256,384]{1,0:T(8,128)(2,1)S(1)} %collective-permute-done.1), channel_id=1, source_target_pairs={{0,2},{2,4},{4,6},{6,8},{8,10},{10,12},{12,14},{14,16},{16,18},{18... | collective-permute-start | bytes 589832 | tf_op jit(solution)/shard_map/ppermute | solution.py:16
  55.6 29.9 %copy-start.11 = (bf16[256,384]{1,0:T(8,128)(2,1)S(1)}, bf16[256,384]{1,0:T(8,128)(2,1)}, u32[]{:S(2)}) copy-start(bf16[256,384]{1,0:T(8,128)(2,1)} %copy-done.10) | copy-start | bytes 589828
  55.6 30.0 %copy-start.9 = (bf16[256,384]{1,0:T(8,128)(2,1)S(1)}, bf16[256,384]{1,0:T(8,128)(2,1)}, u32[]{:S(2)}) copy-start(bf16[256,384]{1,0:T(8,128)(2,1)} %copy-done.8) | copy-start | bytes 589828
  67.7 10.6 %collective-permute-start.14 = (bf16[256,384]{1,0:T(8,128)(2,1)S(1)}, bf16[256,384]{1,0:T(8,128)(2,1)S(1)}, u32[]{:S(2)}, u32[]{:S(2)}) collective-permute-start(bf16[256,384]{1,0:T(8,128)(2,1)S(1)} %collective-permute-done.13), channel_id=1, source_target_pairs={{2,0},{4,2},{6,4},{8,6},{10,8},{12,10},{14,12},{16,14},{18,16},{20... | collective-permute-start | bytes 589832 | tf_op jit(solution)/shard_map/ppermute | solution.py:16
  69.0 10.6 %collective-permute-start.10 = (bf16[256,384]{1,0:T(8,128)(2,1)S(1)}, bf16[256,384]{1,0:T(8,128)(2,1)S(1)}, u32[]{:S(2)}, u32[]{:S(2)}) collective-permute-start(bf16[256,384]{1,0:T(8,128)(2,1)S(1)} %collective-permute-done.9), channel_id=1, source_target_pairs={{0,2},{2,4},{4,6},{6,8},{8,10},{10,12},{12,14},{14,16},{16,18},{18... | collective-permute-start | bytes 589832 | tf_op jit(solution)/shard_map/ppermute | solution.py:16
  72.1 11.8 %collective-permute-start.6 = (bf16[256,384]{1,0:T(8,128)(2,1)S(1)}, bf16[256,384]{1,0:T(8,128)(2,1)S(1)}, u32[]{:S(2)}, u32[]{:S(2)}) collective-permute-start(bf16[256,384]{1,0:T(8,128)(2,1)S(1)} %collective-permute-done.5), channel_id=1, source_target_pairs={{2,0},{4,2},{6,4},{8,6},{10,8},{12,10},{14,12},{16,14},{18,16},{20... | collective-permute-start | bytes 589832 | tf_op jit(solution)/shard_map/ppermute | solution.py:16
  73.4 12.0 %collective-permute-start.3 = (bf16[256,384]{1,0:T(8,128)(2,1)S(1)}, bf16[256,384]{1,0:T(8,128)(2,1)S(1)}, u32[]{:S(2)}, u32[]{:S(2)}) collective-permute-start(bf16[256,384]{1,0:T(8,128)(2,1)S(1)} %collective-permute-done.2), channel_id=1, source_target_pairs={{0,2},{2,4},{4,6},{6,8},{8,10},{10,12},{12,14},{14,16},{16,18},{18... | collective-permute-start | bytes 589832 | tf_op jit(solution)/shard_map/ppermute | solution.py:16
  78.3 20.8 %collective-permute-start.15 = (bf16[256,384]{1,0:T(8,128)(2,1)S(1)}, bf16[256,384]{1,0:T(8,128)(2,1)S(1)}, u32[]{:S(2)}, u32[]{:S(2)}) collective-permute-start(bf16[256,384]{1,0:T(8,128)(2,1)S(1)} %collective-permute-done.14), channel_id=1, source_target_pairs={{2,0},{4,2},{6,4},{8,6},{10,8},{12,10},{14,12},{16,14},{18,16},{20... | collective-permute-start | bytes 589832 | tf_op jit(solution)/shard_map/ppermute | solution.py:16
  79.6 16.8 %collective-permute-start.11 = (bf16[256,384]{1,0:T(8,128)(2,1)S(1)}, bf16[256,384]{1,0:T(8,128)(2,1)S(1)}, u32[]{:S(2)}, u32[]{:S(2)}) collective-permute-start(bf16[256,384]{1,0:T(8,128)(2,1)S(1)} %collective-permute-done.10), channel_id=1, source_target_pairs={{0,2},{2,4},{4,6},{6,8},{8,10},{10,12},{12,14},{14,16},{16,18},{18... | collective-permute-start | bytes 589832 | tf_op jit(solution)/shard_map/ppermute | solution.py:16
  83.9 5.2 %collective-permute-start.7 = (bf16[256,384]{1,0:T(8,128)(2,1)S(1)}, bf16[256,384]{1,0:T(8,128)(2,1)S(1)}, u32[]{:S(2)}, u32[]{:S(2)}) collective-permute-start(bf16[256,384]{1,0:T(8,128)(2,1)S(1)} %collective-permute-done.6), channel_id=1, source_target_pairs={{2,0},{4,2},{6,4},{8,6},{10,8},{12,10},{14,12},{16,14},{18,16},{20... | collective-permute-start | bytes 589832 | tf_op jit(solution)/shard_map/ppermute | solution.py:16
  95.2 2.3 copy-start.7
  114.4 32.1 %collective-permute-start.24 = (f32[256,384]{0,1:T(8,128)S(1)}, f32[256,384]{0,1:T(8,128)S(1)}, u32[]{:S(2)}, u32[]{:S(2)}) collective-permute-start(f32[256,384]{0,1:T(8,128)S(1)} %get-tuple-element.36), channel_id=1, source_target_pairs={{0,2},{2,4},{4,6},{6,8},{8,10},{10,12},{12,14},{14,16},{16,18},{18... | collective-permute-start | bytes 1179656 | tf_op jit(solution)/shard_map/ppermute | solution.py:16
  121.4 25.1 %collective-permute-start.28 = (f32[256,384]{0,1:T(8,128)S(1)}, f32[256,384]{0,1:T(8,128)S(1)}, u32[]{:S(2)}, u32[]{:S(2)}) collective-permute-start(f32[256,384]{0,1:T(8,128)S(1)} %get-tuple-element.37), channel_id=1, source_target_pairs={{2,0},{4,2},{6,4},{8,6},{10,8},{12,10},{14,12},{16,14},{18,16},{20... | collective-permute-start | bytes 1179656 | tf_op jit(solution)/shard_map/ppermute | solution.py:16
  124.9 8.3 %collective-permute-start.16 = (f32[256,384]{0,1:T(8,128)S(1)}, f32[256,384]{0,1:T(8,128)S(1)}, u32[]{:S(2)}, u32[]{:S(2)}) collective-permute-start(f32[256,384]{0,1:T(8,128)S(1)} %get-tuple-element.44), channel_id=1, source_target_pairs={{0,2},{2,4},{4,6},{6,8},{8,10},{10,12},{12,14},{14,16},{16,18},{18... | collective-permute-start | bytes 1179656 | tf_op jit(solution)/shard_map/ppermute | solution.py:16
  127.9 7.8 %collective-permute-start.20 = (f32[256,384]{0,1:T(8,128)S(1)}, f32[256,384]{0,1:T(8,128)S(1)}, u32[]{:S(2)}, u32[]{:S(2)}) collective-permute-start(f32[256,384]{0,1:T(8,128)S(1)} %get-tuple-element.45), channel_id=1, source_target_pairs={{2,0},{4,2},{6,4},{8,6},{10,8},{12,10},{14,12},{16,14},{18,16},{20... | collective-permute-start | bytes 1179656 | tf_op jit(solution)/shard_map/ppermute | solution.py:16
  135.9 15.1 %collective-permute-start.17 = (f32[256,384]{0,1:T(8,128)S(1)}, f32[256,384]{0,1:T(8,128)S(1)}, u32[]{:S(2)}, u32[]{:S(2)}) collective-permute-start(f32[256,384]{0,1:T(8,128)S(1)} %get-tuple-element.42), channel_id=1, source_target_pairs={{0,2},{2,4},{4,6},{6,8},{8,10},{10,12},{12,14},{14,16},{16,18},{18... | collective-permute-start | bytes 1179656 | tf_op jit(solution)/shard_map/ppermute | solution.py:16
  143.8 7.2 %collective-permute-start.21 = (f32[256,384]{0,1:T(8,128)S(1)}, f32[256,384]{0,1:T(8,128)S(1)}, u32[]{:S(2)}, u32[]{:S(2)}) collective-permute-start(f32[256,384]{0,1:T(8,128)S(1)} %get-tuple-element.43), channel_id=1, source_target_pairs={{2,0},{4,2},{6,4},{8,6},{10,8},{12,10},{14,12},{16,14},{18,16},{20... | collective-permute-start | bytes 1179656 | tf_op jit(solution)/shard_map/ppermute | solution.py:16
  146.6 12.8 %collective-permute-start.25 = (f32[256,384]{0,1:T(8,128)S(1)}, f32[256,384]{0,1:T(8,128)S(1)}, u32[]{:S(2)}, u32[]{:S(2)}) collective-permute-start(f32[256,384]{0,1:T(8,128)S(1)} %get-tuple-element.34), channel_id=1, source_target_pairs={{0,2},{2,4},{4,6},{6,8},{8,10},{10,12},{12,14},{14,16},{16,18},{18... | collective-permute-start | bytes 1179656 | tf_op jit(solution)/shard_map/ppermute | solution.py:16
  149.6 9.8 %collective-permute-start.29 = (f32[256,384]{0,1:T(8,128)S(1)}, f32[256,384]{0,1:T(8,128)S(1)}, u32[]{:S(2)}, u32[]{:S(2)}) collective-permute-start(f32[256,384]{0,1:T(8,128)S(1)} %get-tuple-element.35), channel_id=1, source_target_pairs={{2,0},{4,2},{6,4},{8,6},{10,8},{12,10},{14,12},{16,14},{18,16},{20... | collective-permute-start | bytes 1179656 | tf_op jit(solution)/shard_map/ppermute | solution.py:16
  151.1 15.7 %collective-permute-start.18 = (f32[256,384]{0,1:T(8,128)S(1)}, f32[256,384]{0,1:T(8,128)S(1)}, u32[]{:S(2)}, u32[]{:S(2)}) collective-permute-start(f32[256,384]{0,1:T(8,128)S(1)} %get-tuple-element.40), channel_id=1, source_target_pairs={{0,2},{2,4},{4,6},{6,8},{8,10},{10,12},{12,14},{14,16},{16,18},{18... | collective-permute-start | bytes 1179656 | tf_op jit(solution)/shard_map/ppermute | solution.py:16
  156.7 10.1 %collective-permute-start.22 = (f32[256,384]{0,1:T(8,128)S(1)}, f32[256,384]{0,1:T(8,128)S(1)}, u32[]{:S(2)}, u32[]{:S(2)}) collective-permute-start(f32[256,384]{0,1:T(8,128)S(1)} %get-tuple-element.41), channel_id=1, source_target_pairs={{2,0},{4,2},{6,4},{8,6},{10,8},{12,10},{14,12},{16,14},{18,16},{20... | collective-permute-start | bytes 1179656 | tf_op jit(solution)/shard_map/ppermute | solution.py:16
  159.5 16.3 %collective-permute-start.26 = (f32[256,384]{0,1:T(8,128)S(1)}, f32[256,384]{0,1:T(8,128)S(1)}, u32[]{:S(2)}, u32[]{:S(2)}) collective-permute-start(f32[256,384]{0,1:T(8,128)S(1)} %get-tuple-element.32), channel_id=1, source_target_pairs={{0,2},{2,4},{4,6},{6,8},{8,10},{10,12},{12,14},{14,16},{16,18},{18... | collective-permute-start | bytes 1179656 | tf_op jit(solution)/shard_map/ppermute | solution.py:16
  165.5 10.4 %collective-permute-start.30 = (f32[256,384]{0,1:T(8,128)S(1)}, f32[256,384]{0,1:T(8,128)S(1)}, u32[]{:S(2)}, u32[]{:S(2)}) collective-permute-start(f32[256,384]{0,1:T(8,128)S(1)} %get-tuple-element.33), channel_id=1, source_target_pairs={{2,0},{4,2},{6,4},{8,6},{10,8},{12,10},{14,12},{16,14},{18,16},{20... | collective-permute-start | bytes 1179656 | tf_op jit(solution)/shard_map/ppermute | solution.py:16
  166.9 16.7 %collective-permute-start.19 = (f32[256,384]{0,1:T(8,128)S(1)}, f32[256,384]{0,1:T(8,128)S(1)}, u32[]{:S(2)}, u32[]{:S(2)}) collective-permute-start(f32[256,384]{0,1:T(8,128)S(1)} %get-tuple-element.38), channel_id=1, source_target_pairs={{0,2},{2,4},{4,6},{6,8},{8,10},{10,12},{12,14},{14,16},{16,18},{18... | collective-permute-start | bytes 1179656 | tf_op jit(solution)/shard_map/ppermute | solution.py:16
  173.9 9.7 %collective-permute-start.23 = (f32[256,384]{0,1:T(8,128)S(1)}, f32[256,384]{0,1:T(8,128)S(1)}, u32[]{:S(2)}, u32[]{:S(2)}) collective-permute-start(f32[256,384]{0,1:T(8,128)S(1)} %get-tuple-element.39), channel_id=1, source_target_pairs={{2,0},{4,2},{6,4},{8,6},{10,8},{12,10},{14,12},{16,14},{18,16},{20... | collective-permute-start | bytes 1179656 | tf_op jit(solution)/shard_map/ppermute | solution.py:16
  175.8 8.6 %copy-start.2 = (bf16[1536,384]{1,0:T(8,128)(2,1)S(1)}, bf16[1536,384]{1,0:T(8,128)(2,1)}, u32[]{:S(2)}) copy-start(bf16[1536,384]{1,0:T(8,128)(2,1)} %param.17) | copy-start | bytes 3538948
  176.0 9.1 %collective-permute-start.27 = (f32[256,384]{0,1:T(8,128)S(1)}, f32[256,384]{0,1:T(8,128)S(1)}, u32[]{:S(2)}, u32[]{:S(2)}) collective-permute-start(f32[256,384]{0,1:T(8,128)S(1)} %get-tuple-element.30), channel_id=1, source_target_pairs={{0,2},{2,4},{4,6},{6,8},{8,10},{10,12},{12,14},{14,16},{16,18},{18... | collective-permute-start | bytes 1179656 | tf_op jit(solution)/shard_map/ppermute | solution.py:16
  182.3 5.6 %collective-permute-start.31 = (f32[256,384]{0,1:T(8,128)S(1)}, f32[256,384]{0,1:T(8,128)S(1)}, u32[]{:S(2)}, u32[]{:S(2)}) collective-permute-start(f32[256,384]{0,1:T(8,128)S(1)} %get-tuple-element.31), channel_id=1, source_target_pairs={{2,0},{4,2},{6,4},{8,6},{10,8},{12,10},{14,12},{16,14},{18,16},{20... | collective-permute-start | bytes 1179656 | tf_op jit(solution)/shard_map/ppermute | solution.py:16
  184.4 4.2 %copy-start.3 = (bf16[1536,384]{1,0:T(8,128)(2,1)S(1)}, bf16[1536,384]{1,0:T(8,128)(2,1)}, u32[]{:S(2)}) copy-start(bf16[1536,384]{1,0:T(8,128)(2,1)} %param.18) | copy-start | bytes 3538948
  188.6 1.9 copy-start.5
  190.5 152.7 %reduce-scatter.7.cloned.1.call-start = ((), (), s32[]{:S(2)}) async-start(), calls=%async_computation.3 | async-start | bytes 10027008
Sparse Core Ops, SparseCore 0:
  190.6 36.4 reduce-scatter.4
  231.7 111.3 reduce-scatter.6
where the time goes:
time: 353 us; the launch traced here: 352 us
  waiting for transfers between devices  134 us (38%)
  starting transfers between devices  101 us (29%)
  matrix products  42.7 us (12%)
  blocking collectives  25 us (7%)
  other arithmetic  17.3 us (5%)
  between operations  15.7 us (4%)
  local copies, waits for them, and re-layouts  15.3 us (4%)
    unnamed x3, waiting for transfers between devices  114 us
    ppermute x32, starting transfers between devices, passed_along(): lax.ppermute(value, axis, [(source, source + steps) for source in range(f...  101 us
    dot_general x16, matrix products, contract_last(): lax.dot_general(left, right, (((1,), (1,)), ((), ())), preferred_element_...  15 us
    all_gather x1, blocking collectives, body(): lax.all_gather(embedded, 'head', axis=1, tiled=True)  13 us
    dot_general x14, matrix products, contract_first(): lax.dot_general(left, right, (((0,), (0,)), ((), ())), preferred_element_...  12.4 us
    unnamed x43, local copies, waits for them, and re-layouts  12.4 us
    all_gather x1, blocking collectives, body(): lax.all_gather(grad_out, 'head', axis=1, tiled=True)  12.1 us
    reduce_scatter x1, waiting for transfers between devices, body(): lax.psum_scatter(partial_grad, 'head', scatter_dimension=1, tiled=True)  11.3 us
  transfers between devices with their start and end apart: 34, of which 6 were waited for; matrix products, arithmetic and copies ran while one was open for 15% of the time, Pallas kernels for 0%

commit v1 on v0

v1 whole, which is shorter than its diff:
```python
import jax
import jax.numpy as jnp
from jax import lax
from jax.sharding import PartitionSpec as P

HEAD_DIM = 64
HALF = 1024


NEG_FILL = -1e30


def contract_first(left, right):
    return lax.dot_general(
        left, right, (((0,), (0,)), ((), ())), preferred_element_type=jnp.float32
    )


def contract_last(left, right):
    return lax.dot_general(
        left, right, (((1,), (1,)), ((), ())), preferred_element_type=jnp.float32
    )


def swapped(value, axis, bit):
    count = lax.axis_size(axis)
    return lax.ppermute(value, axis, [(source, source ^ bit) for source in range(count)])


def passed_along(value, axis, steps):
    count = lax.axis_size(axis)
    first, last = (max(0, -steps), min(count, count - steps))
    return lax.ppermute(value, axis, [(source, source + steps) for source in range(first, last)])


def picked(array, index, axis):
    return lax.dynamic_index_in_dim(array, index, axis, keepdims=False)


def joined_heads(mine, head_index):
    other = swapped(mine, "head", 1)
    first = jnp.where(head_index == 0, mine, other)
    second = jnp.where(head_index == 0, other, mine)
    return jnp.concatenate([first, second], axis=1)


def summed_rows(part, seq_index):
    count = lax.axis_size("seq")
    groups = count // 4
    rows = part.shape[0] // count
    width = part.shape[1]
    core, side, group = seq_index % 2, seq_index // 2 % 2, seq_index // 4
    blocks = part.reshape(groups, 2, 2, rows, width)
    blocks = picked(blocks, core, 2) + swapped(picked(blocks, 1 - core, 2), "seq", 1)
    sent = picked(blocks, 1 - side, 1).astype(jnp.bfloat16)
    blocks = picked(blocks, side, 1) + swapped(sent, "seq", 2).astype(jnp.float32)
    if groups > 4:
        members = [[g * 4 + place for g in range(groups)] for place in range(4)]
        return lax.psum_scatter(
            blocks.reshape(groups * rows, width),
            "seq",
            scatter_dimension=0,
            axis_index_groups=members,
            tiled=True,
        )
    narrow = blocks.astype(jnp.bfloat16)
    total = picked(blocks, group, 0)
    for distance in range(1, groups):
        for step in (distance, -distance):
            target = jnp.clip(group + step, 0, groups - 1)
            arrived = passed_along(picked(narrow, target, 0), "seq", 4 * step)
            total = total + arrived.astype(jnp.float32)
    return total


def body(
    embedded, grad_out, mask_pos, timestep, time_table, mask_embed, w_query, w_key, w_value, w_out
):
    seq_index = lax.axis_index("seq")
    seq_count = lax.axis_size("seq")
    head_place = lax.axis_index("head")
    core, side = seq_index % 2, seq_index // 2 % 2
    slab_rows = embedded.shape[0]
    total_len = slab_rows * seq_count
    scale = HEAD_DIM ** (-0.5)
    full_rows = joined_heads(embedded, head_place)
    full_grad = joined_heads(grad_out, head_place)
    positions = seq_index * slab_rows + jnp.arange(slab_rows, dtype=jnp.int32)
    masked = jnp.any(positions[:, None] == mask_pos[None, :], axis=1)
    time_row = lax.dynamic_slice_in_dim(time_table, timestep[0], 1, 0).astype(jnp.float32)
    hidden = (
        jnp.where(
            masked[:, None], mask_embed.astype(jnp.float32)[None, :], full_rows.astype(jnp.float32)
        )
        + time_row
    ).astype(jnp.bfloat16)
    key_rows = jnp.dot(hidden, w_key, preferred_element_type=jnp.float32).astype(jnp.bfloat16)
    value_rows = jnp.dot(hidden, w_value, preferred_element_type=jnp.float32).astype(jnp.bfloat16)
    queries = jnp.dot(hidden, w_query, preferred_element_type=jnp.float32).astype(jnp.bfloat16)
    grad_attn = contract_last(full_grad, w_out).astype(jnp.bfloat16)
    group_width = queries.shape[1]
    head_count = group_width // HEAD_DIM

    own = jnp.concatenate([key_rows, value_rows], axis=1)
    below = passed_along(own, "seq", 4)
    above = passed_along(own, "seq", -4)
    plane_side = swapped(own, "seq", 2)
    plane_core = swapped(own, "seq", 1)
    far_side = swapped(jnp.where(side == 1, below, above), "seq", 2)
    far_core = swapped(jnp.where(core == 1, below, above), "seq", 1)
    plane_both = swapped(plane_side, "seq", 1)
    far_both = swapped(far_side, "seq", 1)
    slabs = jnp.concatenate(
        [far_both, plane_both, far_core, plane_core, far_side, plane_side, own, below, above],
        axis=0,
    )
    core_step = 4 - 8 * (1 - core)
    side_step = 4 - 8 * (1 - side)
    numbers = [
        (seq_index ^ 3) + side_step,
        seq_index ^ 3,
        (seq_index ^ 1) + core_step,
        seq_index ^ 1,
        (seq_index ^ 2) + side_step,
        seq_index ^ 2,
        seq_index,
        seq_index - 4,
        seq_index + 4,
    ]
    offsets = jnp.arange(slab_rows, dtype=jnp.int32)
    key_pos = jnp.concatenate([number * slab_rows + offsets for number in numbers])
    keys_all = slabs[:, :group_width]
    values_all = slabs[:, group_width:]
    distance_grid = positions[:, None] - key_pos[None, :]
    band = (
        (jnp.abs(distance_grid) <= HALF) & (key_pos[None, :] >= 0) & (key_pos[None, :] < total_len)
    )
    head_outputs = []
    query_grads = []
    key_grads = []
    value_grads = []
    for head_index in range(head_count):
        lower_col = head_index * HEAD_DIM
        upper_col = lower_col + HEAD_DIM
        head_query = queries[:, lower_col:upper_col]
        head_keys = keys_all[:, lower_col:upper_col]
        head_values = values_all[:, lower_col:upper_col]
        head_grad = grad_attn[:, lower_col:upper_col]
        scores = contract_last(head_query, head_keys) * scale
        scores = jnp.where(band, scores, NEG_FILL)
        row_max = jnp.max(scores, axis=1, keepdims=True)
        log_total = row_max + jnp.log(jnp.sum(jnp.exp(scores - row_max), axis=1, keepdims=True))
        attention = jnp.exp(scores - log_total)
        rounded = attention.astype(jnp.bfloat16)
        output = jnp.dot(rounded, head_values, preferred_element_type=jnp.float32).astype(
            jnp.bfloat16
        )
        head_outputs.append(output)
        delta = jnp.sum(head_grad.astype(jnp.float32) * output.astype(jnp.float32), axis=1)
        dprob = contract_last(head_grad, head_values)
        dscore = (attention * (dprob - delta[:, None])).astype(jnp.bfloat16)
        query_grads.append(scale * jnp.dot(dscore, head_keys, preferred_element_type=jnp.float32))
        key_grads.append(scale * contract_first(dscore, head_query))
        value_grads.append(contract_first(rounded, head_grad))
    attn_out = jnp.concatenate(head_outputs, axis=1)
    query_rounded = jnp.concatenate(query_grads, axis=1).astype(jnp.bfloat16)
    slab_grads = jnp.concatenate(key_grads + value_grads, axis=1)

    def slab_of(first, count):
        return slab_grads[first * slab_rows : (first + count) * slab_rows]

    by_core = swapped(slab_of(0, 4), "seq", 1)
    for_side = by_core[: 2 * slab_rows] + slab_of(4, 2)
    by_side = swapped(for_side, "seq", 2).astype(jnp.float32)
    core_far, core_own = by_core[2 * slab_rows : 3 * slab_rows], by_core[3 * slab_rows :]
    side_far, side_own = by_side[:slab_rows], by_side[slab_rows:]
    to_below = slab_of(7, 1) + jnp.where(core == 1, core_far, 0.0) + jnp.where(side == 1, side_far, 0.0)
    to_above = slab_of(8, 1) + jnp.where(core == 0, core_far, 0.0) + jnp.where(side == 0, side_far, 0.0)
    slab_total = slab_of(6, 1) + core_own + side_own
    slab_total = slab_total + passed_along(to_below, "seq", -4).astype(jnp.float32)
    slab_total = slab_total + passed_along(to_above, "seq", 4).astype(jnp.float32)
    pair_rounded = slab_total.astype(jnp.bfloat16)

    early = summed_rows(
        jnp.concatenate(
            [contract_first(hidden, query_rounded), contract_first(full_grad, attn_out)], axis=1
        ),
        seq_index,
    )
    late = summed_rows(contract_first(hidden, pair_rounded), seq_index)
    partial_grad = contract_last(query_rounded, w_query)
    partial_grad = partial_grad + contract_last(pair_rounded[:, :group_width], w_key)
    partial_grad = partial_grad + contract_last(pair_rounded[:, group_width:], w_value)
    half = embedded.shape[1]
    left, right = partial_grad[:, :half], partial_grad[:, half:]
    kept = jnp.where(head_place == 0, left, right)
    summed = kept + swapped(jnp.where(head_place == 0, right, left), "head", 1)
    input_grad = jnp.where(masked[:, None], 0.0, summed).astype(jnp.bfloat16)
    return (
        input_grad,
        early[:, :group_width],
        late[:, :group_width],
        late[:, group_width:],
        early[:, group_width:],
    )


def solution(mesh):
    placed = (
        P("seq", "head"),
        P("seq", "head"),
        P("seq"),
        P(),
        P(),
        P(),
        P(None, "head"),
        P(None, "head"),
        P(None, "head"),
        P("head", None),
    )
    return jax.shard_map(
        body,
        mesh=mesh,
        in_specs=placed,
        out_specs=(
            P("seq", "head"),
            P("seq", "head"),
            P("seq", "head"),
            P("seq", "head"),
            P("seq", "head"),
        ),
        check_vma=False,
    )
```

time: 353 us -> 241 us (0.68)
  waiting for transfers between devices: 134 us -> 61.3 us
  starting transfers between devices: 101 us -> 72.4 us
  blocking collectives: 25 us -> 0 us
  other arithmetic: 17.3 us -> 34.2 us
  between operations: 15.7 us -> 2.72 us
  local copies, waits for them, and re-layouts: 15.3 us -> 27.7 us
  matrix products: 42.7 us -> 38.2 us
    unnamed x3 -> x0, waiting for transfers between devices: 114 us -> none
    ppermute x0 -> x15, waiting for transfers between devices: none -> 43.5 us  [swapped(): lax.ppermute(value, axis, [(source, source ^ bit) for source in range(cou...]
    ppermute x32 -> x16, starting transfers between devices: 101 us -> 58.6 us  [passed_along(): lax.ppermute(value, axis, [(source, source + steps) for source in range(f...]
    all_gather x2 -> x0, blocking collectives: 25 us -> none  [the longest x1 13 us: body(): lax.all_gather(embedded, 'head', axis=1, tiled=True)]
    ppermute x0 -> x15, starting transfers between devices: none -> 13.8 us  [swapped(): lax.ppermute(value, axis, [(source, source ^ bit) for source in range(cou...]
    add x7 -> x5, other arithmetic: 0.62 us -> 12.3 us  [the longest x2 4.75 us: summed_rows(): picked(blocks, core, 2) + swapped(picked(blocks, 1 - core, 2), 'seq', 1)]
    reduce_scatter x1 -> x0, waiting for transfers between devices: 11.3 us -> none  [body(): lax.psum_scatter(partial_grad, 'head', scatter_dimension=1, tiled=True)]
    ppermute x32 -> x16, waiting for transfers between devices: 8.95 us -> 17.8 us  [passed_along(): lax.ppermute(value, axis, [(source, source + steps) for source in range(f...]
  transfers between devices with their start and end apart: 34 -> 31, of which waited for: 6 -> 10; matrix products, arithmetic and copies ran while one was open for 15% -> 25% of each run, Pallas kernels for 0% -> 0%
where the time goes in v1:
time: 241 us; the launch traced here: 236 us
  starting transfers between devices  72.4 us (30%)
  waiting for transfers between devices  61.3 us (25%)
  matrix products  38.2 us (16%)
  other arithmetic  34.2 us (14%)
  local copies, waits for them, and re-layouts  27.7 us (11%)
  between operations  2.72 us (1%)
    ppermute x16, starting transfers between devices, passed_along(): lax.ppermute(value, axis, [(source, source + steps) for source in range(f...  58.6 us
    ppermute x15, waiting for transfers between devices, swapped(): lax.ppermute(value, axis, [(source, source ^ bit) for source in range(cou...  43.5 us
    ppermute x16, waiting for transfers between devices, passed_along(): lax.ppermute(value, axis, [(source, source + steps) for source in range(f...  17.8 us
    ppermute x15, starting transfers between devices, swapped(): lax.ppermute(value, axis, [(source, source ^ bit) for source in range(cou...  13.8 us
    dot_general x16, matrix products, contract_last(): lax.dot_general(left, right, (((1,), (1,)), ((), ())), preferred_element_...  13 us
    dot_general x6, matrix products, body(): jnp.dot(dscore, head_keys, preferred_element_type=jnp.float32)  9.63 us
    unnamed x102, local copies, waits for them, and re-layouts  9.47 us
    dot_general x15, matrix products, contract_first(): lax.dot_general(left, right, (((0,), (0,)), ((), ())), preferred_element_...  8.26 us
  transfers between devices with their start and end apart: 31, of which 10 were waited for; matrix products, arithmetic and copies ran while one was open for 25% of the time, Pallas kernels for 0%

profile of v1, /device:TPU:0, one launch (start us, length us, event | category | flops | bytes accessed | tf_op | source)
XLA Modules:
  0.0 236.4 jit_solution(10342740836377245847)
XLA Ops:
  0.7 1.3 copy.76
  2.0 3.0 %collective-permute-start = (bf16[256,768]{0,1:T(8,128)(2,1)S(1)}, bf16[256,768]{0,1:T(8,128)(2,1)}, u32[]{:S(2)}, u32[]{:S(2)}) collective-permute-start(bf16[256,768]{0,1:T(8,128)(2,1)S(1)} %copy.76), channel_id=1, source_target_pairs={{0,1},{1,0},{2,3},{3,2},{4,5},{5,4},{6,7},{7,6},{8,9},{9,8},{10,11... | collective-permute-start | bytes 1179656 | tf_op jit(solution)/shard_map/ppermute | solution.py:27
  6.8 1.3 constant_dynamic-update-slice_fusion
  8.1 1.3 constant_dynamic-update-slice_fusion.10
  9.4 1.3 constant_dynamic-update-slice_fusion.11
  12.8 1.3 constant_dynamic-update-slice_fusion.17
  14.2 1.3 constant_dynamic-update-slice_fusion.16
  20.0 4.0 %collective-permute-start.1 = (bf16[256,768]{0,1:T(8,128)(2,1)S(1)}, bf16[256,768]{0,1:T(8,128)(2,1)S(1)}, u32[]{:S(2)}, u32[]{:S(2)}) collective-permute-start(bf16[256,768]{0,1:T(8,128)(2,1)S(1)} %pad_maximum_fusion.4), channel_id=1, source_target_pairs={{0,8},{2,10},{4,12},{6,14},{8,16},{10,18},{12,20},{14,22},{16,24},... | collective-permute-start | bytes 1179656 | tf_op jit(solution)/shard_map/ppermute | solution.py:33
  24.0 1.8 collective-permute-start.2
  25.8 1.6 collective-permute-start.5
  27.4 4.4 %collective-permute-done.1 = bf16[256,768]{0,1:T(8,128)(2,1)S(1)} collective-permute-done((bf16[256,768]{0,1:T(8,128)(2,1)S(1)}, bf16[256,768]{0,1:T(8,128)(2,1)S(1)}, u32[]{:S(2)}, u32[]{:S(2)}) %collective-permute-start.1) | collective-permute-done | bytes 393248 | tf_op jit(solution)/shard_map/ppermute | solution.py:33
  31.8 4.1 %collective-permute-done.2 = bf16[256,768]{0,1:T(8,128)(2,1)S(1)} collective-permute-done((bf16[256,768]{0,1:T(8,128)(2,1)S(1)}, bf16[256,768]{0,1:T(8,128)(2,1)S(1)}, u32[]{:S(2)}, u32[]{:S(2)}) %collective-permute-start.2) | collective-permute-done | bytes 393248 | tf_op jit(solution)/shard_map/ppermute | solution.py:33
  35.9 1.6 collective-permute-start.3
  38.2 6.9 %collective-permute-done.3 = bf16[256,768]{0,1:T(8,128)(2,1)S(1)} collective-permute-done((bf16[256,768]{0,1:T(8,128)(2,1)S(1)}, bf16[256,768]{0,1:T(8,128)(2,1)S(1)}, u32[]{:S(2)}, u32[]{:S(2)}) %collective-permute-start.3) | collective-permute-done | bytes 393248 | tf_op jit(solution)/shard_map/ppermute | solution.py:27
  72.7 2.9 %copy-done.9 = f32[2304,768]{0,1:T(8,128)} copy-done((f32[2304,768]{0,1:T(8,128)}, f32[2304,768]{0,1:T(8,128)S(1)}, u32[]{:S(2)}) %copy-start.9) | copy-done | bytes 7077912
  75.6 2.1 slice.207
  78.1 1.8 concatenate.43
  79.9 1.8 fusion.33
  81.7 1.8 fusion.35
  83.7 2.4 %slice_add_fusion = f32[512,768]{0,1:T(8,128)S(1)} fusion(f32[2304,768]{0,1:T(8,128)} %copy-done.9, f32[1024,768]{0,1:T(8,128)} %collective-permute-done.10), kind=kLoop, calls=%fused_computation.76 | loop fusion | flops 393216 | bytes 4718592 | tf_op jit(solution)/shard_map/add | solution.py:173
  86.1 1.6 collective-permute-start.11
  87.7 1.5 fusion.37
  89.2 1.5 fusion.39
  90.7 1.5 fusion.41
  92.2 1.5 fusion.43
  95.4 27.5 %collective-permute-done.11 = f32[512,768]{0,1:T(8,128)S(1)} collective-permute-done((f32[512,768]{0,1:T(8,128)S(1)}, f32[512,768]{0,1:T(8,128)S(1)}, u32[]{:S(2)}, u32[]{:S(2)}) %collective-permute-start.11) | collective-permute-done | bytes 1572896 | tf_op jit(solution)/shard_map/ppermute | solution.py:27
  122.9 3.3 %fusion.45 = (f32[256,768]{0,1:T(8,128)}, f32[256,768]{0,1:T(8,128)S(1)}) fusion(f32[2304,768]{0,1:T(8,128)} %copy-done.9, f32[512,768]{0,1:T(8,128)S(1)} %collective-permute-done.11, f32[1024,768]{0,1:T(8,128)} %collective-permute-done.10, pred[]{:T(512)S(6)} %eq.47, pred[]{:T(512)S(6)} %eq.46, pred[]{:T(512)S(6)} %eq.49, pred[]{:T(512)S(6)} %eq.48), kind=kLoop, calls=%fused_computation.113 | loop fusion | flops 1572864 | bytes 4718596 | tf_op jit(solution)/shard_map/add | solution.py:177
  127.5 5.5 %collective-permute-start.13 = (f32[256,768]{0,1:T(8,128)S(1)}, f32[256,768]{0,1:T(8,128)}, u32[]{:S(2)}, u32[]{:S(2)}) collective-permute-start(f32[256,768]{0,1:T(8,128)S(1)} %get-tuple-element.21), channel_id=1, source_target_pairs={{0,8},{2,10},{4,12},{6,14},{8,16},{10,18},{12,20},{14,22},{16,24},... | collective-permute-start | bytes 2359304 | tf_op jit(solution)/shard_map/ppermute | solution.py:33
  133.0 2.4 %pad_maximum_fusion = f32[1536,768]{0,1:T(8,128)} fusion(f32[1536,384]{0,1:T(8,128)S(1)} %fusion.51, f32[1536,384]{0,1:T(8,128)S(1)} %fusion.127), kind=kLoop, calls=%fused_computation | loop fusion | flops 1179648 | bytes 9437184 | tf_op jit(solution)/shard_map/concatenate | solution.py:185
  135.4 6.0 %copy.92 = f32[1536,768]{1,0:T(8,128)} copy(f32[1536,768]{0,1:T(8,128)} %pad_maximum_fusion) | data formatting | bytes 9437184 | tf_op jit(solution)/shard_map/concatenate | solution.py:185
  141.4 3.3 %dynamic-slice_bitcast_fusion.1 = f32[4,2,96,768]{3,2,1,0:T(8,128)} fusion(f32[4,2,2,96,768]{4,3,2,1,0:T(8,128)} %bitcast.99, s32[]{:T(128)S(6)} %select_n.189), kind=kLoop, calls=%fused_computation.54 | loop fusion | bytes 4718596 | tf_op jit(solution)/shard_map/jit(dynamic_index_in_dim)/squeeze | solution.py:37
  144.8 2.8 %collective-permute-done.12 = f32[256,768]{0,1:T(8,128)} collective-permute-done((f32[256,768]{0,1:T(8,128)}, f32[256,768]{0,1:T(8,128)}, u32[]{:S(2)}, u32[]{:S(2)}) %collective-permute-start.12) | collective-permute-done | bytes 786464 | tf_op jit(solution)/shard_map/ppermute | solution.py:33
  148.4 2.1 fusion.48
  151.6 1.6 dynamic-slice_bitcast_fusion
  155.0 2.8 %bitcast_add_fusion.1 = f32[4,2,96,768]{3,2,1,0:T(8,128)S(1)} fusion(f32[4,2,96,768]{3,2,1,0:T(8,128)} %collective-permute-done.15, f32[4,2,2,96,768]{4,3,2,1,0:T(8,128)} %bitcast.100, s32[]{:T(128)S(6)} %select_n.188), kind=kLoop, calls=%fused_computation.52 | loop fusion | flops 589824 | bytes 7077892 | tf_op jit(solution)/shard_map/add | solution.py:54
  157.9 1.6 collective-permute-start.16
  160.7 2.0 bitcast_add_fusion
  162.7 1.4 collective-permute-start.24
  164.2 1.6 collective-permute-start.14
  165.7 8.3 %collective-permute-done.16 = bf16[4,96,768]{2,1,0:T(8,128)(2,1)S(1)} collective-permute-done((bf16[4,96,768]{2,1,0:T(8,128)(2,1)S(1)}, bf16[4,96,768]{2,1,0:T(8,128)(2,1)S(1)}, u32[]{:S(2)}, u32[]{:S(2)}) %collective-permute-start.16) | collective-permute-done | bytes 589856 | tf_op jit(solution)/shard_map/ppermute | solution.py:27
  176.0 4.5 %collective-permute-start.17 = (bf16[96,768]{1,0:T(8,128)(2,1)S(1)}, bf16[96,768]{1,0:T(8,128)(2,1)S(1)}, u32[]{:S(2)}, u32[]{:S(2)}) collective-permute-start(bf16[96,768]{1,0:T(8,128)(2,1)S(1)} %get-tuple-element.34), channel_id=1, source_target_pairs={{0,8},{2,10},{4,12},{6,14},{8,16},{10,18},{12,20},{14,22},{16,24},... | collective-permute-start | bytes 442376 | tf_op jit(solution)/shard_map/ppermute | solution.py:33
  181.8 6.0 %collective-permute-start.19 = (bf16[96,768]{1,0:T(8,128)(2,1)S(1)}, bf16[96,768]{1,0:T(8,128)(2,1)S(1)}, u32[]{:S(2)}, u32[]{:S(2)}) collective-permute-start(bf16[96,768]{1,0:T(8,128)(2,1)S(1)} %get-tuple-element.38), channel_id=1, source_target_pairs={{0,16},{2,18},{4,20},{6,22},{8,24},{10,26},{12,28},{14,30},{1,17},... | collective-permute-start | bytes 442376 | tf_op jit(solution)/shard_map/ppermute | solution.py:33
  190.3 8.2 %collective-permute-start.21 = (bf16[96,768]{1,0:T(8,128)(2,1)}, bf16[96,768]{1,0:T(8,128)(2,1)}, u32[]{:S(2)}, u32[]{:S(2)}) collective-permute-start(bf16[96,768]{1,0:T(8,128)(2,1)} %get-tuple-element.36), channel_id=1, source_target_pairs={{0,24},{2,26},{4,28},{6,30},{1,25},{3,27},{5,29},{7,31}} | collective-permute-start | bytes 442376 | tf_op jit(solution)/shard_map/ppermute | solution.py:33
  201.4 1.9 collective-permute-start.25
  204.7 8.8 %collective-permute-start.27 = (bf16[96,768]{1,0:T(8,128)(2,1)}, bf16[96,768]{1,0:T(8,128)(2,1)}, u32[]{:S(2)}, u32[]{:S(2)}) collective-permute-start(bf16[96,768]{1,0:T(8,128)(2,1)} %get-tuple-element.32), channel_id=1, source_target_pairs={{0,16},{2,18},{4,20},{6,22},{8,24},{10,26},{12,28},{14,30},{1,17},... | collective-permute-start | bytes 442376 | tf_op jit(solution)/shard_map/ppermute | solution.py:33
  214.8 9.0 %collective-permute-start.29 = (bf16[96,768]{1,0:T(8,128)(2,1)}, bf16[96,768]{1,0:T(8,128)(2,1)}, u32[]{:S(2)}, u32[]{:S(2)}) collective-permute-start(bf16[96,768]{1,0:T(8,128)(2,1)} %get-tuple-element.30), channel_id=1, source_target_pairs={{0,24},{2,26},{4,28},{6,30},{1,25},{3,27},{5,29},{7,31}} | collective-permute-start | bytes 442376 | tf_op jit(solution)/shard_map/ppermute | solution.py:33
  227.3 5.6 %collective-permute-done.30 = bf16[96,768]{1,0:T(8,128)(2,1)} collective-permute-done((bf16[96,768]{1,0:T(8,128)(2,1)}, bf16[96,768]{1,0:T(8,128)(2,1)}, u32[]{:S(2)}, u32[]{:S(2)}) %collective-permute-start.30) | collective-permute-done | bytes 147488 | tf_op jit(solution)/shard_map/ppermute | solution.py:33
  232.9 1.8 fusion.56
  (218 shorter events, 60.2 us)
Async XLA Ops:
  0.6 44.5 %copy-start = (bf16[1536,384]{1,0:T(8,128)(2,1)S(1)}, bf16[1536,384]{1,0:T(8,128)(2,1)}, u32[]{:S(2)}) copy-start(bf16[1536,384]{1,0:T(8,128)(2,1)} %param.16) | copy-start | bytes 3538948
  0.6 16.7 %copy-start.20 = (bf16[1536,384]{1,0:T(8,128)(2,1)S(1)}, bf16[1536,384]{1,0:T(8,128)(2,1)}, u32[]{:S(2)}) copy-start(bf16[1536,384]{1,0:T(8,128)(2,1)} %param.17) | copy-start | bytes 3538948
  2.0 14.3 %collective-permute-start = (bf16[256,768]{0,1:T(8,128)(2,1)S(1)}, bf16[256,768]{0,1:T(8,128)(2,1)}, u32[]{:S(2)}, u32[]{:S(2)}) collective-permute-start(bf16[256,768]{0,1:T(8,128)(2,1)S(1)} %copy.76), channel_id=1, source_target_pairs={{0,1},{1,0},{2,3},{3,2},{4,5},{5,4},{6,7},{7,6},{8,9},{9,8},{10,11... | collective-permute-start | bytes 1179656 | tf_op jit(solution)/shard_map/ppermute | solution.py:27
  6.1 31.4 %collective-permute-start.9 = (bf16[256,768]{0,1:T(8,128)(2,1)S(1)}, bf16[256,768]{0,1:T(8,128)(2,1)S(1)}, u32[]{:S(2)}, u32[]{:S(2)}) collective-permute-start(bf16[256,768]{0,1:T(8,128)(2,1)S(1)} %copy.81), channel_id=1, source_target_pairs={{0,1},{1,0},{2,3},{3,2},{4,5},{5,4},{6,7},{7,6},{8,9},{9,8},{10,11... | collective-permute-start | bytes 1179656 | tf_op jit(solution)/shard_map/ppermute | solution.py:27
  16.2 28.9 %copy-start.38 = (pred[256]{0:T(512)(128)(4,1)}, pred[256]{0:T(512)(128)(4,1)S(1)}, u32[]{:S(2)}) copy-start(pred[256]{0:T(512)(128)(4,1)S(1)} %compare_reduce_fusion) | copy-start | bytes 772
  17.3 27.8 %copy-start.10 = (bf16[256,768]{0,1:T(8,128)(2,1)}, bf16[256,768]{0,1:T(8,128)(2,1)S(1)}, u32[]{:S(2)}) copy-start(bf16[256,768]{0,1:T(8,128)(2,1)S(1)} %get-tuple-element.26) | copy-start | bytes 1179652
  17.3 27.8 %copy-start.12 = (bf16[256,768]{0,1:T(8,128)(2,1)}, bf16[256,768]{0,1:T(8,128)(2,1)S(1)}, u32[]{:S(2)}) copy-start(bf16[256,768]{0,1:T(8,128)(2,1)S(1)} %get-tuple-element.27) | copy-start | bytes 1179652
  18.9 6.9 %copy-start.37 = (s32[2304]{0:T(1024)S(1)}, s32[2304]{0:T(1024)}, u32[]{:S(2)}) copy-start(s32[2304]{0:T(1024)} %constant_dynamic-update-slice_fusion.16) | copy-start | bytes 27652
  20.0 11.8 %collective-permute-start.1 = (bf16[256,768]{0,1:T(8,128)(2,1)S(1)}, bf16[256,768]{0,1:T(8,128)(2,1)S(1)}, u32[]{:S(2)}, u32[]{:S(2)}) collective-permute-start(bf16[256,768]{0,1:T(8,128)(2,1)S(1)} %pad_maximum_fusion.4), channel_id=1, source_target_pairs={{0,8},{2,10},{4,12},{6,14},{8,16},{10,18},{12,20},{14,22},{16,24},... | collective-permute-start | bytes 1179656 | tf_op jit(solution)/shard_map/ppermute | solution.py:33
  24.0 11.9 %collective-permute-start.2 = (bf16[256,768]{0,1:T(8,128)(2,1)S(1)}, bf16[256,768]{0,1:T(8,128)(2,1)S(1)}, u32[]{:S(2)}, u32[]{:S(2)}) collective-permute-start(bf16[256,768]{0,1:T(8,128)(2,1)S(1)} %pad_maximum_fusion.4), channel_id=1, source_target_pairs={{8,0},{10,2},{12,4},{14,6},{16,8},{18,10},{20,12},{22,14},{24,16},... | collective-permute-start | bytes 1179656 | tf_op jit(solution)/shard_map/ppermute | solution.py:33
  25.8 11.9 %collective-permute-start.5 = (bf16[256,768]{0,1:T(8,128)(2,1)S(1)}, bf16[256,768]{0,1:T(8,128)(2,1)S(1)}, u32[]{:S(2)}, u32[]{:S(2)}) collective-permute-start(bf16[256,768]{0,1:T(8,128)(2,1)S(1)} %pad_maximum_fusion.4), channel_id=1, source_target_pairs={{0,4},{2,6},{4,0},{6,2},{8,12},{10,14},{12,8},{14,10},{16,20},{18,... | collective-permute-start | bytes 1179656 | tf_op jit(solution)/shard_map/ppermute | solution.py:27
  35.9 9.2 %collective-permute-start.3 = (bf16[256,768]{0,1:T(8,128)(2,1)S(1)}, bf16[256,768]{0,1:T(8,128)(2,1)S(1)}, u32[]{:S(2)}, u32[]{:S(2)}) collective-permute-start(bf16[256,768]{0,1:T(8,128)(2,1)S(1)} %get-tuple-element.25), channel_id=1, source_target_pairs={{0,4},{2,6},{4,0},{6,2},{8,12},{10,14},{12,8},{14,10},{16,20},{18,... | collective-permute-start | bytes 1179656 | tf_op jit(solution)/shard_map/ppermute | solution.py:27
  37.5 10.8 %collective-permute-start.8 = (bf16[256,768]{0,1:T(8,128)(2,1)S(1)}, bf16[256,768]{0,1:T(8,128)(2,1)S(1)}, u32[]{:S(2)}, u32[]{:S(2)}) collective-permute-start(bf16[256,768]{0,1:T(8,128)(2,1)S(1)} %pad_maximum_fusion.4), channel_id=1, source_target_pairs={{0,2},{2,0},{4,6},{6,4},{8,10},{10,8},{12,14},{14,12},{16,18},{18,... | collective-permute-start | bytes 1179656 | tf_op jit(solution)/shard_map/ppermute | solution.py:27
  37.6 10.0 %copy-start.14 = (bf16[256,768]{0,1:T(8,128)(2,1)}, bf16[256,768]{0,1:T(8,128)(2,1)S(1)}, u32[]{:S(2)}) copy-start(bf16[256,768]{0,1:T(8,128)(2,1)S(1)} %get-tuple-element.22) | copy-start | bytes 1179652
  37.6 10.0 %copy-start.16 = (bf16[256,768]{0,1:T(8,128)(2,1)}, bf16[256,768]{0,1:T(8,128)(2,1)S(1)}, u32[]{:S(2)}) copy-start(bf16[256,768]{0,1:T(8,128)(2,1)S(1)} %get-tuple-element.23) | copy-start | bytes 1179652
  37.6 9.3 %copy-start.43 = (bf16[384,1536]{1,0:T(8,128)(2,1)S(1)}, bf16[384,1536]{1,0:T(8,128)(2,1)}, u32[]{:S(2)}) copy-start(bf16[384,1536]{1,0:T(8,128)(2,1)} %param.19) | copy-start | bytes 3538948
  37.7 10.0 %collective-permute-start.6 = (bf16[256,768]{0,1:T(8,128)(2,1)S(1)}, bf16[256,768]{0,1:T(8,128)(2,1)S(1)}, u32[]{:S(2)}, u32[]{:S(2)}) collective-permute-start(bf16[256,768]{0,1:T(8,128)(2,1)S(1)} %collective-permute-done.5), channel_id=1, source_target_pairs={{0,2},{2,0},{4,6},{6,4},{8,10},{10,8},{12,14},{14,12},{16,18},{18,... | collective-permute-start | bytes 1179656 | tf_op jit(solution)/shard_map/ppermute | solution.py:27
  45.1 2.5 %collective-permute-start.4 = (bf16[256,768]{0,1:T(8,128)(2,1)S(1)}, bf16[256,768]{0,1:T(8,128)(2,1)S(1)}, u32[]{:S(2)}, u32[]{:S(2)}) collective-permute-start(bf16[256,768]{0,1:T(8,128)(2,1)S(1)} %collective-permute-done.3), channel_id=1, source_target_pairs={{0,2},{2,0},{4,6},{6,4},{8,10},{10,8},{12,14},{14,12},{16,18},{18,... | collective-permute-start | bytes 1179656 | tf_op jit(solution)/shard_map/ppermute | solution.py:27
  46.4 1.9 collective-permute-start.7
  48.6 17.7 %copy-start.8 = (bf16[2304,768]{0,1:T(8,128)(2,1)}, bf16[2304,768]{0,1:T(8,128)(2,1)S(1)}, u32[]{:S(2)}) copy-start(bf16[2304,768]{0,1:T(8,128)(2,1)S(1)} %constant_dynamic-update-slice_fusion.1) | copy-start | bytes 10616836
  77.7 6.0 %collective-permute-start.10 = (f32[1024,768]{0,1:T(8,128)}, f32[1024,768]{0,1:T(8,128)}, u32[]{:S(2)}, u32[]{:S(2)}) collective-permute-start(f32[1024,768]{0,1:T(8,128)} %slice.207), channel_id=1, source_target_pairs={{0,2},{2,0},{4,6},{6,4},{8,10},{10,8},{12,14},{14,12},{16,18},{18,... | collective-permute-start | bytes 9437192 | tf_op jit(solution)/shard_map/ppermute | solution.py:27
  83.6 5.6 %copy-start.3 = (bf16[256,2304]{1,0:T(8,128)(2,1)S(1)}, bf16[256,2304]{1,0:T(8,128)(2,1)}, u32[]{:S(2)}) copy-start(bf16[256,2304]{1,0:T(8,128)(2,1)} %copy-done.2) | copy-start | bytes 3538948
  86.1 36.8 %collective-permute-start.11 = (f32[512,768]{0,1:T(8,128)S(1)}, f32[512,768]{0,1:T(8,128)S(1)}, u32[]{:S(2)}, u32[]{:S(2)}) collective-permute-start(f32[512,768]{0,1:T(8,128)S(1)} %slice_add_fusion), channel_id=1, source_target_pairs={{0,4},{2,6},{4,0},{6,2},{8,12},{10,14},{12,8},{14,10},{16,20},{18,... | collective-permute-start | bytes 4718600 | tf_op jit(solution)/shard_map/ppermute | solution.py:27
  126.2 21.3 %collective-permute-start.12 = (f32[256,768]{0,1:T(8,128)}, f32[256,768]{0,1:T(8,128)}, u32[]{:S(2)}, u32[]{:S(2)}) collective-permute-start(f32[256,768]{0,1:T(8,128)} %get-tuple-element.20), channel_id=1, source_target_pairs={{8,0},{10,2},{12,4},{14,6},{16,8},{18,10},{20,12},{22,14},{24,16},... | collective-permute-start | bytes 2359304 | tf_op jit(solution)/shard_map/ppermute | solution.py:33
  127.5 20.9 %collective-permute-start.13 = (f32[256,768]{0,1:T(8,128)S(1)}, f32[256,768]{0,1:T(8,128)}, u32[]{:S(2)}, u32[]{:S(2)}) collective-permute-start(f32[256,768]{0,1:T(8,128)S(1)} %get-tuple-element.21), channel_id=1, source_target_pairs={{0,8},{2,10},{4,12},{6,14},{8,16},{10,18},{12,20},{14,22},{16,24},... | collective-permute-start | bytes 2359304 | tf_op jit(solution)/shard_map/ppermute | solution.py:33
  141.4 7.0 %copy-start.19 = (f32[512,768]{0,1:T(8,128)S(1)}, f32[512,768]{0,1:T(8,128)}, u32[]{:S(2)}) copy-start(f32[512,768]{0,1:T(8,128)} %copy-done.18) | copy-start | bytes 4718596
  144.8 5.8 %copy-start.40 = (pred[256]{0:T(512)(128)(4,1)S(1)}, pred[256]{0:T(512)(128)(4,1)}, u32[]{:S(2)}) copy-start(pred[256]{0:T(512)(128)(4,1)} %copy-done.38) | copy-start | bytes 772
  144.8 10.3 %collective-permute-start.15 = (f32[4,2,96,768]{3,2,1,0:T(8,128)}, f32[4,2,96,768]{3,2,1,0:T(8,128)}, u32[]{:S(2)}, u32[]{:S(2)}) collective-permute-start(f32[4,2,96,768]{3,2,1,0:T(8,128)} %dynamic-slice_bitcast_fusion.1), channel_id=1, source_target_pairs={{0,2},{2,0},{4,6},{6,4},{8,10},{10,8},{12,14},{14,12},{16,18},{18,... | collective-permute-start | bytes 7077896 | tf_op jit(solution)/shard_map/ppermute | solution.py:27
  154.4 6.2 %collective-permute-start.23 = (f32[4,2,96,768]{3,2,1,0:T(8,128)}, f32[4,2,96,768]{3,2,1,0:T(8,128)}, u32[]{:S(2)}, u32[]{:S(2)}) collective-permute-start(f32[4,2,96,768]{3,2,1,0:T(8,128)} %dynamic-slice_bitcast_fusion), channel_id=1, source_target_pairs={{0,2},{2,0},{4,6},{6,4},{8,10},{10,8},{12,14},{14,12},{16,18},{18,... | collective-permute-start | bytes 7077896 | tf_op jit(solution)/shard_map/ppermute | solution.py:27
  157.9 16.2 %collective-permute-start.16 = (bf16[4,96,768]{2,1,0:T(8,128)(2,1)S(1)}, bf16[4,96,768]{2,1,0:T(8,128)(2,1)S(1)}, u32[]{:S(2)}, u32[]{:S(2)}) collective-permute-start(bf16[4,96,768]{2,1,0:T(8,128)(2,1)S(1)} %fusion.49), channel_id=1, source_target_pairs={{0,4},{2,6},{4,0},{6,2},{8,12},{10,14},{12,8},{14,10},{16,20},{18,... | collective-permute-start | bytes 1769480 | tf_op jit(solution)/shard_map/ppermute | solution.py:27
  162.7 25.1 %collective-permute-start.24 = (bf16[4,96,768]{2,1,0:T(8,128)(2,1)S(1)}, bf16[4,96,768]{2,1,0:T(8,128)(2,1)S(1)}, u32[]{:S(2)}, u32[]{:S(2)}) collective-permute-start(bf16[4,96,768]{2,1,0:T(8,128)(2,1)S(1)} %fusion.50), channel_id=1, source_target_pairs={{0,4},{2,6},{4,0},{6,2},{8,12},{10,14},{12,8},{14,10},{16,20},{18,... | collective-permute-start | bytes 1769480 | tf_op jit(solution)/shard_map/ppermute | solution.py:27
  164.2 50.6 %collective-permute-start.14 = (f32[256,768]{0,1:T(8,128)S(1)}, f32[256,768]{0,1:T(8,128)}, u32[]{:S(2)}, u32[]{:S(2)}) collective-permute-start(f32[256,768]{0,1:T(8,128)S(1)} %slice_select_fusion), channel_id=1, source_target_pairs={{0,1},{1,0},{2,3},{3,2},{4,5},{5,4},{6,7},{7,6},{8,9},{9,8},{10,11... | collective-permute-start | bytes 2359304 | tf_op jit(solution)/shard_map/ppermute | solution.py:27
  176.0 14.3 %collective-permute-start.17 = (bf16[96,768]{1,0:T(8,128)(2,1)S(1)}, bf16[96,768]{1,0:T(8,128)(2,1)S(1)}, u32[]{:S(2)}, u32[]{:S(2)}) collective-permute-start(bf16[96,768]{1,0:T(8,128)(2,1)S(1)} %get-tuple-element.34), channel_id=1, source_target_pairs={{0,8},{2,10},{4,12},{6,14},{8,16},{10,18},{12,20},{14,22},{16,24},... | collective-permute-start | bytes 442376 | tf_op jit(solution)/shard_map/ppermute | solution.py:33
  180.5 18.0 %collective-permute-start.18 = (bf16[96,768]{1,0:T(8,128)(2,1)S(1)}, bf16[96,768]{1,0:T(8,128)(2,1)S(1)}, u32[]{:S(2)}, u32[]{:S(2)}) collective-permute-start(bf16[96,768]{1,0:T(8,128)(2,1)S(1)} %get-tuple-element.39), channel_id=1, source_target_pairs={{8,0},{10,2},{12,4},{14,6},{16,8},{18,10},{20,12},{22,14},{24,16},... | collective-permute-start | bytes 442376 | tf_op jit(solution)/shard_map/ppermute | solution.py:33
  181.8 18.9 %collective-permute-start.19 = (bf16[96,768]{1,0:T(8,128)(2,1)S(1)}, bf16[96,768]{1,0:T(8,128)(2,1)S(1)}, u32[]{:S(2)}, u32[]{:S(2)}) collective-permute-start(bf16[96,768]{1,0:T(8,128)(2,1)S(1)} %get-tuple-element.38), channel_id=1, source_target_pairs={{0,16},{2,18},{4,20},{6,22},{8,24},{10,26},{12,28},{14,30},{1,17},... | collective-permute-start | bytes 442376 | tf_op jit(solution)/shard_map/ppermute | solution.py:33
  187.8 37.2 %copy-start.41 = (pred[256]{0:T(512)(128)(4,1)S(1)}, pred[256]{0:T(512)(128)(4,1)}, u32[]{:S(2)}) copy-start(pred[256]{0:T(512)(128)(4,1)} %copy-done.38) | copy-start | bytes 772
  187.9 15.5 %collective-permute-start.20 = (bf16[96,768]{1,0:T(8,128)(2,1)}, bf16[96,768]{1,0:T(8,128)(2,1)}, u32[]{:S(2)}, u32[]{:S(2)}) collective-permute-start(bf16[96,768]{1,0:T(8,128)(2,1)} %get-tuple-element.37), channel_id=1, source_target_pairs={{16,0},{18,2},{20,4},{22,6},{24,8},{26,10},{28,12},{30,14},{17,1},... | collective-permute-start | bytes 442376 | tf_op jit(solution)/shard_map/ppermute | solution.py:33
  190.3 10.4 %copy-start.32 = (bf16[96,768]{1,0:T(8,128)(2,1)}, bf16[96,768]{1,0:T(8,128)(2,1)S(1)}, u32[]{:S(2)}) copy-start(bf16[96,768]{1,0:T(8,128)(2,1)S(1)} %collective-permute-done.17) | copy-start | bytes 442372
  190.3 14.3 %collective-permute-start.21 = (bf16[96,768]{1,0:T(8,128)(2,1)}, bf16[96,768]{1,0:T(8,128)(2,1)}, u32[]{:S(2)}, u32[]{:S(2)}) collective-permute-start(bf16[96,768]{1,0:T(8,128)(2,1)} %get-tuple-element.36), channel_id=1, source_target_pairs={{0,24},{2,26},{4,28},{6,30},{1,25},{3,27},{5,29},{7,31}} | collective-permute-start | bytes 442376 | tf_op jit(solution)/shard_map/ppermute | solution.py:33
  198.5 15.0 %collective-permute-start.22 = (bf16[96,768]{1,0:T(8,128)(2,1)}, bf16[96,768]{1,0:T(8,128)(2,1)}, u32[]{:S(2)}, u32[]{:S(2)}) collective-permute-start(bf16[96,768]{1,0:T(8,128)(2,1)} %get-tuple-element.35), channel_id=1, source_target_pairs={{24,0},{26,2},{28,4},{30,6},{25,1},{27,3},{29,5},{31,7}} | collective-permute-start | bytes 442376 | tf_op jit(solution)/shard_map/ppermute | solution.py:33
  201.4 22.3 %collective-permute-start.25 = (bf16[96,768]{1,0:T(8,128)(2,1)}, bf16[96,768]{1,0:T(8,128)(2,1)}, u32[]{:S(2)}, u32[]{:S(2)}) collective-permute-start(bf16[96,768]{1,0:T(8,128)(2,1)} %get-tuple-element.28), channel_id=1, source_target_pairs={{0,8},{2,10},{4,12},{6,14},{8,16},{10,18},{12,20},{14,22},{16,24},... | collective-permute-start | bytes 442376 | tf_op jit(solution)/shard_map/ppermute | solution.py:33
  203.4 23.9 %collective-permute-start.26 = (bf16[96,768]{1,0:T(8,128)(2,1)}, bf16[96,768]{1,0:T(8,128)(2,1)}, u32[]{:S(2)}, u32[]{:S(2)}) collective-permute-start(bf16[96,768]{1,0:T(8,128)(2,1)} %get-tuple-element.33), channel_id=1, source_target_pairs={{8,0},{10,2},{12,4},{14,6},{16,8},{18,10},{20,12},{22,14},{24,16},... | collective-permute-start | bytes 442376 | tf_op jit(solution)/shard_map/ppermute | solution.py:33
  204.7 22.6 %collective-permute-start.27 = (bf16[96,768]{1,0:T(8,128)(2,1)}, bf16[96,768]{1,0:T(8,128)(2,1)}, u32[]{:S(2)}, u32[]{:S(2)}) collective-permute-start(bf16[96,768]{1,0:T(8,128)(2,1)} %get-tuple-element.32), channel_id=1, source_target_pairs={{0,16},{2,18},{4,20},{6,22},{8,24},{10,26},{12,28},{14,30},{1,17},... | collective-permute-start | bytes 442376 | tf_op jit(solution)/shard_map/ppermute | solution.py:33
  213.5 13.8 %collective-permute-start.28 = (bf16[96,768]{1,0:T(8,128)(2,1)}, bf16[96,768]{1,0:T(8,128)(2,1)}, u32[]{:S(2)}, u32[]{:S(2)}) collective-permute-start(bf16[96,768]{1,0:T(8,128)(2,1)} %get-tuple-element.31), channel_id=1, source_target_pairs={{16,0},{18,2},{20,4},{22,6},{24,8},{26,10},{28,12},{30,14},{17,1},... | collective-permute-start | bytes 442376 | tf_op jit(solution)/shard_map/ppermute | solution.py:33
  214.8 18.1 %copy-start.33 = (bf16[96,768]{1,0:T(8,128)(2,1)S(1)}, bf16[96,768]{1,0:T(8,128)(2,1)}, u32[]{:S(2)}) copy-start(bf16[96,768]{1,0:T(8,128)(2,1)} %copy-done.32) | copy-start | bytes 442372
  214.8 18.1 %copy-start.35 = (bf16[96,768]{1,0:T(8,128)(2,1)S(1)}, bf16[96,768]{1,0:T(8,128)(2,1)}, u32[]{:S(2)}) copy-start(bf16[96,768]{1,0:T(8,128)(2,1)} %copy-done.34) | copy-start | bytes 442372
  214.8 12.5 %collective-permute-start.29 = (bf16[96,768]{1,0:T(8,128)(2,1)}, bf16[96,768]{1,0:T(8,128)(2,1)}, u32[]{:S(2)}, u32[]{:S(2)}) collective-permute-start(bf16[96,768]{1,0:T(8,128)(2,1)} %get-tuple-element.30), channel_id=1, source_target_pairs={{0,24},{2,26},{4,28},{6,30},{1,25},{3,27},{5,29},{7,31}} | collective-permute-start | bytes 442376 | tf_op jit(solution)/shard_map/ppermute | solution.py:33
  223.8 9.1 %collective-permute-start.30 = (bf16[96,768]{1,0:T(8,128)(2,1)}, bf16[96,768]{1,0:T(8,128)(2,1)}, u32[]{:S(2)}, u32[]{:S(2)}) collective-permute-start(bf16[96,768]{1,0:T(8,128)(2,1)} %get-tuple-element.29), channel_id=1, source_target_pairs={{24,0},{26,2},{28,4},{30,6},{25,1},{27,3},{29,5},{31,7}} | collective-permute-start | bytes 442376 | tf_op jit(solution)/shard_map/ppermute | solution.py:33
  (29 other events, 74.9 us)
